TPU v7x, 128 devices: a whole 4x4x4 slice. The times are simulated.
128 devices in a mesh: item: 32 (over y, x, core), user: 4 (over z).
Axes of the slice: x: 4, y: 4, z: 4, core: 2. Of those that a mesh axis runs over, the one named last changes fastest.
Arguments:
- tiles: float32 [768, 32, 128, 128], P('user', 'item'), may hold values from -6 to 6
- tile_user: int32 [768, 32], P('user', 'item'), may hold values from 0 to 31
- tile_item: int32 [768, 32], P('user', 'item'), may hold values from 0 to 127
- row_lengths: int32 [768, 32, 128], P('user', 'item'), may hold values from 1 to 128
- start_panel: float32 [524288, 64], P('item'), may hold values from -6 to 6
Outputs:
- panel: float32 [524288, 64], P('item')
All inputs are finite; a program needn't handle non-finite values.
Results may differ from a plain program's by a relative error of at most 0.0003.
Values sent between devices are 32-bit elements; how exact they have to be, the bound alone decides.
No kernel may reach another device: no remote copies, remote signals or barrier semaphores. Data moves between devices by JAX's collectives and lax.ppermute only.
A program may use at most 128 MiB of HBM per device.

v0:
```python
import functools

import jax
import jax.numpy as jnp
from jax import lax
from jax.experimental import pallas as pl
from jax.experimental.pallas import tpu as pltpu
from jax.sharding import PartitionSpec as P

ITERS = 2
TB = 128
K = 64
NT = 192
IB = 128
UB = 32
QB = 32
HB = 16
ITEMS = 524288
GROUP = 48
RUN = 16
VMEM = pl.BlockSpec(memory_space=pltpu.VMEM)
SMEM = pl.BlockSpec(memory_space=pltpu.SMEM)
ANY = pl.BlockSpec(memory_space=pl.ANY)
MIB = 1024 * 1024
F32, BF16 = jnp.float32, jnp.bfloat16


def cost(us):
    return pl.CostEstimate(flops=0, bytes_accessed=int(us * 3.5e6), transcendentals=0)


def split2(x):
    hi = x.astype(BF16)
    lo = (x - hi.astype(F32)).astype(BF16)
    return hi, lo


def split3(x):
    hi = x.astype(BF16)
    rest = x - hi.astype(F32)
    mid = rest.astype(BF16)
    lo = (rest - mid.astype(F32)).astype(BF16)
    return hi, mid, lo


def times_nt(block, stacked):
    left = jnp.concatenate(split2(block), axis=0)
    full = lax.dot_general(left, stacked, (((1,), (1,)), ((), ())), preferred_element_type=F32)
    half = full[:K] + full[K:]
    return half[:, :TB] + half[:, TB:]


def times_nn(block, stacked):
    hi, lo = split2(block)
    left = jnp.concatenate(
        [jnp.concatenate([hi, hi], axis=1), jnp.concatenate([lo, lo], axis=1)], axis=0
    )
    full = lax.dot_general(left, stacked, (((1,), (0,)), ((), ())), preferred_element_type=F32)
    return full[:K] + full[K:]


def place_of(user_block, spot):
    core = (user_block >> 4) ^ (spot & 1)
    x = ((user_block >> 2) - (spot >> 1)) & 3
    y = (user_block - (spot >> 3)) & 3
    return core * 16 + x * 4 + y


def first_kernel(upos, item, tiles, lengths, panel, users, stacked):
    step = pl.program_id(0)

    @pl.when(step == 0)
    def _():
        users[...] = jnp.zeros_like(users)

    columns = lax.broadcasted_iota(jnp.int32, (TB, TB), 1)
    ends = lengths[...].T
    parts = []
    for t in range(GROUP):
        n = step * GROUP + t
        masked = jnp.where(columns < ends[:, t : t + 1], tiles[t], 0.0)
        both = jnp.concatenate(split2(masked), axis=0)
        stacked[t] = both
        block = panel[:, pl.ds(pl.multiple_of(item[n] * TB, TB), TB)]
        parts.append((upos[n], times_nt(block, both)))
    for spot, value in parts:
        users[spot] += value


def first_product(upos, item, tiles, lengths, panel_t):
    return pl.pallas_call(
        first_kernel,
        out_shape=(
            jax.ShapeDtypeStruct((UB, K, TB), F32),
            pltpu.VMEM((NT, 2 * TB, TB), BF16),
        ),
        grid_spec=pltpu.PrefetchScalarGridSpec(
            num_scalar_prefetch=2,
            grid=(NT // GROUP,),
            in_specs=[
                pl.BlockSpec((GROUP, TB, TB), lambda s, *_: (s, 0, 0)),
                pl.BlockSpec((GROUP, TB), lambda s, *_: (s, 0)),
                pl.BlockSpec((K, IB * TB), lambda s, *_: (0, 0)),
            ],
            out_specs=[
                pl.BlockSpec((UB, K, TB), lambda s, *_: (0, 0, 0)),
                pl.BlockSpec((GROUP, 2 * TB, TB), lambda s, *_: (s, 0, 0)),
            ],
        ),
        cost_estimate=cost(13.8),
        compiler_params=pltpu.CompilerParams(vmem_limit_bytes=28 * MIB),
    )(upos, item, tiles, lengths, panel_t)


def each_tile(first, last, lists, stacked, total, use):
    start, end = lists[3 * NT + first], lists[3 * NT + last]

    def step(g, carry):
        parts = []
        for t in range(RUN):
            j = start + g * RUN + t
            at = jnp.minimum(j, end - 1)
            spot, value = use(lists[NT + at], lists[2 * NT + at], stacked[lists[at]])
            parts.append((spot, jnp.where(j < end, value, 0.0)))
        for spot, value in parts:
            total[spot, :K] += value
        return carry

    lax.fori_loop(0, (end - start + RUN - 1) >> 4, step, 0)


def back_kernel(first, last, shift, sizes, lists, users, stacked, *rest):
    outs = rest[: len(sizes)]
    (total,) = rest[len(sizes) :]
    total[...] = jnp.zeros_like(total)

    def use(user, item, tile):
        return item - shift * HB, times_nn(users[user, :K], tile)

    each_tile(first, last, lists, stacked, total, use)
    at = 0
    for size, out in zip(sizes, outs):
        out[...] = total[at : at + size]
        at += size


def back_product(first, last, shift, sizes, lists, users, stacked):
    return pl.pallas_call(
        functools.partial(back_kernel, first, last, shift, sizes),
        out_shape=[jax.ShapeDtypeStruct((size, K, TB), F32) for size in sizes],
        in_specs=[SMEM, VMEM, VMEM],
        out_specs=[VMEM] * len(sizes),
        scratch_shapes=[pltpu.VMEM((sum(sizes), K, TB), F32)],
        cost_estimate=cost(2.5 + 0.04 * sum(sizes)),
        compiler_params=pltpu.CompilerParams(vmem_limit_bytes=8 * MIB),
    )(lists, users, stacked)


def gram_of(blocks):
    total = jnp.zeros((3 * K, 3 * K), F32)
    for first, second in zip(blocks[::2], blocks[1::2]):
        three = jnp.concatenate(split3(jnp.concatenate([first, second], axis=1)), axis=0)
        total += lax.dot_general(three, three, (((1,), (1,)), ((), ())), preferred_element_type=F32)
    rows = (total[2 * K :] + total[K : 2 * K]) + total[:K]
    return (rows[:, 2 * K :] + rows[:, K : 2 * K]) + rows[:, :K]


def forth_kernel(first, last, shift, count, more, final, lists, stacked, *rest):
    ins = rest[:count]
    rest = rest[count:]
    if more:
        before, gram_before, rest = rest[0], rest[1], rest[2:]
    if final:
        out, panel = rest
        out[...] = jnp.zeros_like(out)
    else:
        out, gram, panel = rest
    out[:, :K] = before[...] if more else jnp.zeros((UB, K, TB), F32)
    for place, piece in enumerate(ins):
        panel[place * HB : (place + 1) * HB] = piece[...]

    def use(user, item, tile):
        return user, times_nt(panel[item - shift * HB], tile)

    own = gram_of([panel[b] for b in range(count * HB)])
    if more:
        own = own + gram_before[...]
    if final:
        for b in range(UB):
            out[lists[PLACE_AT + b], K : K + 2, :K] = own[2 * b : 2 * b + 2]
    else:
        gram[...] = own
    each_tile(first, last, lists, stacked, out, use)


def forth_product(first, last, shift, lists, stacked, pieces, before=None, final=False):
    more = before is not None
    args = list(pieces) + (list(before) if more else [])
    shapes = [jax.ShapeDtypeStruct((UB, K, TB), F32), jax.ShapeDtypeStruct((K, K), F32)]
    if final:
        shapes = [jax.ShapeDtypeStruct((UB, K + 8, TB), F32)]
    return pl.pallas_call(
        functools.partial(forth_kernel, first, last, shift, len(pieces), more, final),
        out_shape=shapes,
        in_specs=[SMEM] + [VMEM] * (1 + len(args)),
        out_specs=[VMEM] * len(shapes),
        scratch_shapes=[pltpu.VMEM((len(pieces) * HB, K, TB), F32)],
        cost_estimate=cost(3.0 + 0.8 * len(pieces)),
        compiler_params=pltpu.CompilerParams(vmem_limit_bytes=8 * MIB),
    )(lists, stacked, *args)


def gram_kernel(own, out):
    out[...] = gram_of([own[b] for b in range(QB)])


def gram_product(own):
    return pl.pallas_call(
        gram_kernel,
        out_shape=jax.ShapeDtypeStruct((K, K), F32),
        in_specs=[VMEM],
        out_specs=VMEM,
        cost_estimate=cost(0.7),
        compiler_params=pltpu.CompilerParams(vmem_limit_bytes=4 * MIB),
    )(own)


def inverse_of(gram):
    rows = lax.broadcasted_iota(jnp.int32, (K, 2 * K), 0)
    lanes = lax.broadcasted_iota(jnp.int32, (K, 2 * K), 1)
    unit = (lanes == rows + K).astype(F32)
    left = gram * F32(1.0 / ITEMS)
    work = jnp.concatenate([left, jnp.zeros((K, K), F32)], axis=1) + unit
    for k in range(K):
        pivot = work[k : k + 1, k : k + 1]
        scaled = work[k : k + 1, :] * lax.rsqrt(pivot)
        column = work[:, k : k + 1] * lax.rsqrt(pivot)
        lower = work - column * scaled
        work = jnp.where(rows > k, lower, jnp.where(rows == k, scaled, work))
    return work[:, K:]


def inverse_kernel(gram, out):
    out[...] = inverse_of(gram[...])


def inverse_lower(gram):
    return pl.pallas_call(
        inverse_kernel,
        out_shape=jax.ShapeDtypeStruct((K, K), F32),
        in_specs=[VMEM],
        out_specs=VMEM,
        cost_estimate=cost(6.7),
        compiler_params=pltpu.CompilerParams(vmem_limit_bytes=2 * MIB),
    )(gram)


def inverse_beside_kernel(lists, users, out, gram):
    for b in range(UB):
        gram[2 * b : 2 * b + 2] = users[lists[PLACE_AT + b], K : K + 2, :K]
    out[...] = inverse_of(gram[...])


def inverse_beside(lists, users):
    return pl.pallas_call(
        inverse_beside_kernel,
        out_shape=jax.ShapeDtypeStruct((K, K), F32),
        in_specs=[SMEM, VMEM],
        out_specs=VMEM,
        scratch_shapes=[pltpu.VMEM((K, K), F32)],
        cost_estimate=cost(6.9),
        compiler_params=pltpu.CompilerParams(vmem_limit_bytes=2 * MIB),
    )(lists, users)


def exact_left(inverse):
    high, mid, low = split3(inverse)
    return jnp.concatenate([high, high, mid, mid], axis=1), jnp.concatenate([high, low], axis=1)


def exact_times(left, block):
    high, mid, low = split3(block)
    large = jnp.concatenate([high, mid, high, mid], axis=0)
    small = jnp.concatenate([low, high], axis=0)
    return jnp.dot(left[1], small, preferred_element_type=F32) + jnp.dot(
        left[0], large, preferred_element_type=F32
    )


def scale_kernel(inverse, *refs):
    left = exact_left(inverse[...])
    out = refs[-1]
    for half in range(2):
        first, second, third = refs[3 * half : 3 * half + 3]
        for b in range(HB):
            out[half * HB + b] = exact_times(left, (first[b] + second[b]) + third[b])


def scale_sum(inverse, terms):
    return pl.pallas_call(
        scale_kernel,
        out_shape=jax.ShapeDtypeStruct((QB, K, TB), F32),
        in_specs=[VMEM] * 7,
        out_specs=VMEM,
        cost_estimate=cost(0.9),
        compiler_params=pltpu.CompilerParams(vmem_limit_bytes=4 * MIB),
    )(inverse, *terms)


def final_kernel(cuts, base, inverse, *refs):
    out, made, sems = refs[-3:]
    left = exact_left(inverse[...])
    copies = []
    for place, (number, start) in enumerate(cuts):
        for b in range(HB):
            made[place, :, b * TB : (b + 1) * TB] = exact_times(left, refs[number][start + b])
        at = pl.multiple_of(base[place], HB * TB)
        copy = pltpu.make_async_copy(
            made.at[place], out.at[:, pl.ds(at, HB * TB)], sems.at[place]
        )
        copy.start()
        copies.append(copy)
    for copy in copies:
        copy.wait()


def final_product(base, inverse, arrays, cuts, before=None):
    more = [] if before is None else [before]
    return pl.pallas_call(
        functools.partial(final_kernel, cuts),
        out_shape=jax.ShapeDtypeStruct((K, IB * TB), F32),
        in_specs=[SMEM] + [VMEM] * (1 + len(arrays)) + [ANY] * len(more),
        out_specs=ANY,
        scratch_shapes=[
            pltpu.VMEM((len(cuts), K, HB * TB), F32),
            pltpu.SemaphoreType.DMA((len(cuts),)),
        ],
        input_output_aliases={2 + len(arrays): 0} if more else {},
        cost_estimate=cost(1.0 + 0.5 * len(cuts)),
        compiler_params=pltpu.CompilerParams(vmem_limit_bytes=8 * MIB),
    )(base, inverse, *arrays, *more)


def user_move(value, by):
    return lax.ppermute(value, "user", [(s, (s + by) % 4) for s in range(4)])


def item_move(value, dy=0, dx=0, dc=0):
    pairs = []
    for y in range(4):
        for x in range(4):
            for c in range(2):
                to = (((y + dy) % 4) * 4 + (x + dx) % 4) * 2 + (c + dc) % 2
                pairs.append(((y * 4 + x) * 2 + c, to))
    return lax.ppermute(value, "item", pairs)


def sum_over_item(part):
    mine = part[:16] + item_move(part[16:], dc=1)
    near, right, far, left = mine[:4], mine[4:8], mine[8:12], mine[12:]
    mine = near + item_move(right, dx=1) + item_move(left, dx=-1) + item_move(far, dx=2)
    one, two, three = item_move(mine, dy=1), item_move(mine, dy=2), item_move(mine, dy=-1)
    mine = (mine + jnp.roll(two, 2, 0)) + (jnp.roll(one, -1, 0) + jnp.roll(three, 1, 0))
    left, far, right = item_move(mine, dx=1), item_move(mine, dx=2), item_move(mine, dx=-1)
    mine = jnp.concatenate([mine, right, far, left], axis=0)
    return jnp.concatenate([mine, item_move(mine, dc=1)], axis=0)


def sum_all_user(value):
    return (value + user_move(value, 2)) + (user_move(value, 1) + user_move(value, -1))


def sum_all_item(value):
    value = value + item_move(value, dc=1)
    value = (value + item_move(value, dx=2)) + (item_move(value, dx=1) + item_move(value, dx=-1))
    return (value + item_move(value, dy=2)) + (item_move(value, dy=1) + item_move(value, dy=-1))


FAR_A, FAR_B, UP_B, DOWN_A, UP_A, DOWN_B, OWN_A, OWN_B = range(8)
PLACES = {0: (OWN_A, OWN_B), 1: (UP_A, UP_B), 2: (FAR_A, FAR_B), 3: (DOWN_A, DOWN_B)}
BOUNDS = (0, UP_B, UP_A, OWN_A, 8)
PLACE_AT = 3 * NT + len(BOUNDS)
LISTS = 640


def scatter(users, lists, stacked):
    far_a, far_b = back_product(0, 1, FAR_A, (HB, HB), lists, users, stacked)
    got_a, got_b = user_move(far_a, 1), user_move(far_b, -1)
    up_b, down_a = back_product(1, 2, UP_B, (HB, HB), lists, users, stacked)
    direct_b, direct_a = user_move(up_b, 1), user_move(down_a, -1)
    up_a, down_b, own_a, own_b = back_product(2, 4, UP_A, (HB,) * 4, lists, users, stacked)
    sum_a, sum_b = user_move(up_a + got_a, 1), user_move(down_b + got_b, -1)
    return lax.optimization_barrier((own_a, direct_a, sum_a, own_b, direct_b, sum_b))


def item_places(item_block, z):
    quarter = (item_block // QB - z) % 4
    half = (item_block // HB) % 2
    place = jnp.zeros_like(quarter)
    for at, (first, second) in PLACES.items():
        place = jnp.where(quarter == at, jnp.where(half == 0, first, second), place)
    return place * HB + item_block % HB


def tile_lists(upos, ipos, places):
    number = jnp.arange(NT, dtype=jnp.int32)
    key = ipos * NT + number
    rank = jnp.sum((key[None, :] < key[:, None]).astype(jnp.int32), axis=1)
    spot = rank[None, :] == number[:, None]

    def sort(values):
        return jnp.sum(jnp.where(spot, values[None, :], 0), axis=1)

    ends = jnp.array(BOUNDS, jnp.int32) * HB
    bounds = jnp.sum((ipos[None, :] < ends[:, None]).astype(jnp.int32), axis=1)
    out = jnp.zeros((LISTS,), jnp.int32)
    at = 0
    for piece in (sort(number), sort(upos), sort(ipos), bounds, places):
        out = out + jnp.pad(piece, (at, LISTS - at - piece.shape[0]))
        at += piece.shape[0]
    return out


def body(tiles, tile_user, tile_item, row_lengths, start_panel):
    tiles = tiles.reshape(NT, TB, TB)
    user_block = tile_user.reshape(NT)
    item_block = tile_item.reshape(NT)
    spot = lax.axis_index("item")
    z = lax.axis_index("user")

    halves = (0, 0), (0, 1), (3, 0), (3, 1), (1, 0), (1, 1), (2, 0), (2, 1)
    quarters, odd = (jnp.array(column, jnp.int32) for column in zip(*halves))
    base = ((z + quarters) % 4) * (QB * TB) + odd * (HB * TB)
    upos, places = place_of(user_block, spot), place_of(jnp.arange(UB, dtype=jnp.int32), spot)
    ipos = item_places(item_block, z)
    upos, ipos, places, base = lax.optimization_barrier((upos, ipos, places, base))
    part, stacked = first_product(upos, item_block, tiles, row_lengths.reshape(NT, TB), start_panel.T)
    lists = tile_lists(upos, ipos, places)
    users = sum_over_item(part)
    terms = scatter(users, lists, stacked)
    own_a, own_b = (terms[0] + terms[1]) + terms[2], (terms[3] + terms[4]) + terms[5]
    down_a, up_b = user_move(own_a, 1), user_move(own_b, -1)
    down_b, up_a = user_move(own_b, 1), user_move(own_a, -1)
    far = user_move(down_a, 1), user_move(up_b, -1)
    before = forth_product(3, 4, OWN_A, lists, stacked, (own_a, own_b))
    before = forth_product(1, 3, UP_B, lists, stacked, (up_b, down_a, up_a, down_b), before)
    (part,) = forth_product(0, 1, FAR_A, lists, stacked, far, before, True)
    users = sum_over_item(part)
    terms = scatter(users, lists, stacked)
    own = scale_sum(inverse_beside(lists, users), terms)
    down, up = user_move(own, 1), user_move(own, -1)
    gram = sum_all_user(sum_all_item(gram_product(own)))
    gram, down, up = lax.optimization_barrier((gram, down, up))
    far = user_move(down[:HB], 1), user_move(up[HB:], -1)
    inverse = inverse_lower(gram)
    cuts = (0, 0), (0, HB), (1, 0), (1, HB), (2, 0), (2, HB)
    panel = final_product(base[:6], inverse, (own, down, up), cuts)
    return final_product(base[6:], inverse, far, ((0, 0), (1, 0)), panel).T


def solution(mesh):
    placed = (
        P("user", "item", None, None),
        P("user", "item"),
        P("user", "item"),
        P("user", "item", None),
        P("item", None),
    )
    return jax.shard_map(
        body, mesh=mesh, in_specs=placed, out_specs=P("item", None), check_vma=False
    )
```

profile of v0, /device:TPU:0, one launch (start us, length us, event | category | flops | bytes accessed | tf_op | source)
XLA Modules:
  0.0 252.4 jit_solution(13432413819599041350)
XLA Ops:
  5.8 8.9 %shard_map.82 = (f32[32,64,128]{2,1,0:T(8,128)S(1)}, bf16[192,256,128]{2,1,0:T(8,128)(2,1)S(1)}) custom-call(s32[192]{0:T(256)S(1)} %bitcast.9, s32[192]{0:T(256)S(1)} %bitcast.12, f32[192,128,128]{2,1,0:T(8,128)} %bitcast.14, s32[192,128]{1,0:T(8,128)S(1)} %bitcast.8, f32[64,16384]{1,0:T(8,128)S(1)} %bitcast.7), custom_call_target="tpu_custom_call" | custom-call | bytes 48300000 | tf_op jit(solution)/shard_map/pallas_call | solution.py:91
  27.6 3.3 %collective-permute-start.4 = (f32[4,64,128]{2,1,0:T(8,128)S(1)}, f32[4,64,128]{2,1,0:T(8,128)S(1)}, u32[]{:S(2)}, u32[]{:S(2)}) collective-permute-start(f32[4,64,128]{2,1,0:T(8,128)S(1)} %fusion.4), channel_id=1, source_target_pairs={{0,64},{4,68},{8,72},{12,76},{16,80},{20,84},{24,88},{28,92},{32,9... | collective-permute-start | bytes 393224 | tf_op jit(solution)/shard_map/ppermute | solution.py:355
  52.1 3.8 %collective-permute-start.15 = (f32[16,64,128]{2,1,0:T(8,128)S(1)}, f32[16,64,128]{2,1,0:T(8,128)S(1)}, u32[]{:S(2)}, u32[]{:S(2)}) collective-permute-start(f32[16,64,128]{2,1,0:T(8,128)S(1)} %get-tuple-element.59), channel_id=1, source_target_pairs={{0,3},{1,0},{2,1},{3,2},{4,7},{5,4},{6,5},{7,6},{8,11},{9,8},{10,9... | collective-permute-start | bytes 1572872 | tf_op jit(solution)/shard_map/ppermute | solution.py:345
  55.9 4.0 %shard_map.83 = (f32[16,64,128]{2,1,0:T(8,128)S(1)}, f32[16,64,128]{2,1,0:T(8,128)S(1)}, f32[16,64,128]{2,1,0:T(8,128)S(1)}, f32[16,64,128]{2,1,0:T(8,128)S(1)}) custom-call(s32[640]{0:T(1024)S(1)} %pad_add_fusion.lists, f32[32,64,128]{2,1,0:T(8,128)S(1)} %constant_dynamic-update-slice_fusion.users, bf16[192,256,128]{2,1,0:T(8,128)(2,1)S(1)} %get-tuple-element.50.stacked), custom_call_target="tpu_custom_call" | custom-call | bytes 17710000 | tf_op jit(solution)/shard_map/pallas_call | solution.py:148
  61.9 3.3 %collective-permute-start.11 = (f32[16,64,128]{2,1,0:T(8,128)S(1)}, f32[16,64,128]{2,1,0:T(8,128)S(1)}, u32[]{:S(2)}, u32[]{:S(2)}) collective-permute-start(f32[16,64,128]{2,1,0:T(8,128)S(1)} %get-tuple-element.53), channel_id=1, source_target_pairs={{0,3},{1,0},{2,1},{3,2},{4,7},{5,4},{6,5},{7,6},{8,11},{9,8},{10,9... | collective-permute-start | bytes 1572872 | tf_op jit(solution)/shard_map/ppermute | solution.py:345
  68.2 3.8 %collective-permute-start.16 = (f32[16,64,128]{2,1,0:T(8,128)S(1)}, f32[16,64,128]{2,1,0:T(8,128)S(1)}, u32[]{:S(2)}, u32[]{:S(2)}) collective-permute-start(f32[16,64,128]{2,1,0:T(8,128)S(1)} %add.192), channel_id=1, source_target_pairs={{0,3},{1,0},{2,1},{3,2},{4,7},{5,4},{6,5},{7,6},{8,11},{9,8},{10,9... | collective-permute-start | bytes 1572872 | tf_op jit(solution)/shard_map/ppermute | solution.py:345
  72.1 7.3 %collective-permute-done.11 = f32[16,64,128]{2,1,0:T(8,128)S(1)} collective-permute-done((f32[16,64,128]{2,1,0:T(8,128)S(1)}, f32[16,64,128]{2,1,0:T(8,128)S(1)}, u32[]{:S(2)}, u32[]{:S(2)}) %collective-permute-start.11) | collective-permute-done | bytes 524320 | tf_op jit(solution)/shard_map/ppermute | solution.py:345
  79.3 3.7 %collective-permute-done.14 = f32[16,64,128]{2,1,0:T(8,128)S(1)} collective-permute-done((f32[16,64,128]{2,1,0:T(8,128)S(1)}, f32[16,64,128]{2,1,0:T(8,128)S(1)}, u32[]{:S(2)}, u32[]{:S(2)}) %collective-permute-start.14) | collective-permute-done | bytes 524320 | tf_op jit(solution)/shard_map/ppermute | solution.py:345
  83.1 7.2 %collective-permute-done.16 = f32[16,64,128]{2,1,0:T(8,128)S(1)} collective-permute-done((f32[16,64,128]{2,1,0:T(8,128)S(1)}, f32[16,64,128]{2,1,0:T(8,128)S(1)}, u32[]{:S(2)}, u32[]{:S(2)}) %collective-permute-start.16) | collective-permute-done | bytes 524320 | tf_op jit(solution)/shard_map/ppermute | solution.py:345
  90.3 3.4 %collective-permute-done.13 = f32[16,64,128]{2,1,0:T(8,128)S(1)} collective-permute-done((f32[16,64,128]{2,1,0:T(8,128)S(1)}, f32[16,64,128]{2,1,0:T(8,128)S(1)}, u32[]{:S(2)}, u32[]{:S(2)}) %collective-permute-start.13) | collective-permute-done | bytes 524320 | tf_op jit(solution)/shard_map/ppermute | solution.py:345
  99.3 9.4 %collective-permute-done.19.rest_0_ = f32[16,64,128]{2,1,0:T(8,128)S(1)} collective-permute-done((f32[16,64,128]{2,1,0:T(8,128)S(1)}, f32[16,64,128]{2,1,0:T(8,128)S(1)}, u32[]{:S(2)}, u32[]{:S(2)}) %collective-permute-start.19) | collective-permute-done | bytes 524320 | tf_op jit(solution)/shard_map/ppermute | solution.py:345
  114.1 7.5 %collective-permute-done.22.rest_3_ = f32[16,64,128]{2,1,0:T(8,128)S(1)} collective-permute-done((f32[16,64,128]{2,1,0:T(8,128)S(1)}, f32[16,64,128]{2,1,0:T(8,128)S(1)}, u32[]{:S(2)}, u32[]{:S(2)}) %collective-permute-start.22) | collective-permute-done | bytes 524320 | tf_op jit(solution)/shard_map/ppermute | solution.py:345
  121.6 4.5 %shard_map.87 = (f32[32,64,128]{2,1,0:T(8,128)S(1)}, f32[64,64]{1,0:T(8,128)S(1)}) custom-call(s32[640]{0:T(1024)S(1)} %pad_add_fusion.lists, bf16[192,256,128]{2,1,0:T(8,128)(2,1)S(1)} %get-tuple-element.50.stacked, f32[16,64,128]{2,1,0:T(8,128)S(1)} %collective-permute-done.19.rest_0_, f32[16,64,128]{2,1,0:T(8,128)S(1)} %collective-permute-done.17.rest_1_, ...), custom_call_target="tpu_custom_call" | custom-call | bytes 21700000 | tf_op jit(solution)/shard_map/pallas_call | solution.py:202
  126.2 3.5 %collective-permute-done.20.rest_1_ = f32[16,64,128]{2,1,0:T(8,128)S(1)} collective-permute-done((f32[16,64,128]{2,1,0:T(8,128)S(1)}, f32[16,64,128]{2,1,0:T(8,128)S(1)}, u32[]{:S(2)}, u32[]{:S(2)}) %collective-permute-start.20) | collective-permute-done | bytes 524320 | tf_op jit(solution)/shard_map/ppermute | solution.py:345
  136.8 3.2 %collective-permute-start.25 = (f32[4,72,128]{2,1,0:T(8,128)S(1)}, f32[4,72,128]{2,1,0:T(8,128)S(1)}, u32[]{:S(2)}, u32[]{:S(2)}) collective-permute-start(f32[4,72,128]{2,1,0:T(8,128)S(1)} %get-tuple-element.96), channel_id=1, source_target_pairs={{0,24},{4,28},{8,0},{12,4},{16,8},{20,12},{24,16},{28,20},{32,56},... | collective-permute-start | bytes 442376 | tf_op jit(solution)/shard_map/ppermute | solution.py:355
  140.0 7.0 %collective-permute-done.24 = f32[4,72,128]{2,1,0:T(8,128)S(1)} collective-permute-done((f32[4,72,128]{2,1,0:T(8,128)S(1)}, f32[4,72,128]{2,1,0:T(8,128)S(1)}, u32[]{:S(2)}, u32[]{:S(2)}) %collective-permute-start.24) | collective-permute-done | bytes 147488 | tf_op jit(solution)/shard_map/ppermute | solution.py:355
  150.4 4.7 %collective-permute-done.28 = f32[4,72,128]{2,1,0:T(8,128)S(1)} collective-permute-done((f32[4,72,128]{2,1,0:T(8,128)S(1)}, f32[4,72,128]{2,1,0:T(8,128)S(1)}, u32[]{:S(2)}, u32[]{:S(2)}) %collective-permute-start.28) | collective-permute-done | bytes 147488 | tf_op jit(solution)/shard_map/ppermute | solution.py:355
  161.1 3.3 %collective-permute-done.30 = f32[4,72,128]{2,1,0:T(8,128)S(1)} collective-permute-done((f32[4,72,128]{2,1,0:T(8,128)S(1)}, f32[4,72,128]{2,1,0:T(8,128)S(1)}, u32[]{:S(2)}, u32[]{:S(2)}) %collective-permute-start.30) | collective-permute-done | bytes 147488 | tf_op jit(solution)/shard_map/ppermute | solution.py:355
  174.9 4.0 %shard_map.90 = (f32[16,64,128]{2,1,0:T(8,128)S(1)}, f32[16,64,128]{2,1,0:T(8,128)S(1)}, f32[16,64,128]{2,1,0:T(8,128)S(1)}, f32[16,64,128]{2,1,0:T(8,128)S(1)}) custom-call(s32[640]{0:T(1024)S(1)} %pad_add_fusion.lists, f32[32,72,128]{2,1,0:T(8,128)S(1)} %constant_dynamic-update-slice_fusion.5.users, bf16[192,256,128]{2,1,0:T(8,128)(2,1)S(1)} %get-tuple-element.50.stacked), custom_call_target="tpu_custom_call" | custom-call | bytes 17710000 | tf_op jit(solution)/shard_map/pallas_call | solution.py:148
  183.0 4.7 %collective-permute-done.38 = f32[16,64,128]{2,1,0:T(8,128)S(1)} collective-permute-done((f32[16,64,128]{2,1,0:T(8,128)S(1)}, f32[16,64,128]{2,1,0:T(8,128)S(1)}, u32[]{:S(2)}, u32[]{:S(2)}) %collective-permute-start.38) | collective-permute-done | bytes 524320 | tf_op jit(solution)/shard_map/ppermute | solution.py:345
  190.2 5.9 %shard_map.89.inverse = f32[64,64]{1,0:T(8,128)S(1)} custom-call(s32[640]{0:T(1024)S(1)} %pad_add_fusion.lists, f32[32,72,128]{2,1,0:T(8,128)S(1)} %constant_dynamic-update-slice_fusion.5.users), custom_call_target="tpu_custom_call" | custom-call | bytes 24150000 | tf_op jit(solution)/shard_map/pallas_call | solution.py:265
  200.2 8.6 %collective-permute-done.39.refs_5_ = f32[16,64,128]{2,1,0:T(8,128)S(1)} collective-permute-done((f32[16,64,128]{2,1,0:T(8,128)S(1)}, f32[16,64,128]{2,1,0:T(8,128)S(1)}, u32[]{:S(2)}, u32[]{:S(2)}) %collective-permute-start.39) | collective-permute-done | bytes 524320 | tf_op jit(solution)/shard_map/ppermute | solution.py:345
  241.0 5.3 %shard_map.95.inverse = f32[64,64]{1,0:T(8,128)S(1)} custom-call(f32[64,64]{1,0:T(8,128)S(1)} %add_add_fusion.2.gram), custom_call_target="tpu_custom_call" | custom-call | bytes 23450000 | tf_op jit(solution)/shard_map/pallas_call | solution.py:248
  246.3 3.3 %shard_map.96.refs_2_ = f32[64,16384]{1,0:T(8,128)} custom-call(s32[6]{0:T(128)S(1)} %bitcast.13, f32[64,64]{1,0:T(8,128)S(1)} %shard_map.95.inverse, f32[32,64,128]{2,1,0:T(8,128)S(1)} %shard_map.93.own.refs_0_, f32[32,64,128]{2,1,0:T(8,128)S(1)} %collective-permute-done.50.refs_1_, f32[32,64,128]{2,1,0:T(8,128)S(1)} %collective-permute-done.51.refs_2_), custom_call_target="tpu_custom_call" | custom-call | bytes 14000000 | tf_op jit(solution)/shard_map/pallas_call | solution.py:329
  (159 shorter events, 128.2 us)
Async XLA Ops:
  52.1 16.0 %collective-permute-start.15 = (f32[16,64,128]{2,1,0:T(8,128)S(1)}, f32[16,64,128]{2,1,0:T(8,128)S(1)}, u32[]{:S(2)}, u32[]{:S(2)}) collective-permute-start(f32[16,64,128]{2,1,0:T(8,128)S(1)} %get-tuple-element.59), channel_id=1, source_target_pairs={{0,3},{1,0},{2,1},{3,2},{4,7},{5,4},{6,5},{7,6},{8,11},{9,8},{10,9... | collective-permute-start | bytes 1572872 | tf_op jit(solution)/shard_map/ppermute | solution.py:345
  55.9 16.1 %collective-permute-start.12 = (f32[16,64,128]{2,1,0:T(8,128)S(1)}, f32[16,64,128]{2,1,0:T(8,128)S(1)}, u32[]{:S(2)}, u32[]{:S(2)}) collective-permute-start(f32[16,64,128]{2,1,0:T(8,128)S(1)} %get-tuple-element.55), channel_id=1, source_target_pairs={{0,1},{1,2},{2,3},{3,0},{4,5},{5,6},{6,7},{7,4},{8,9},{9,10},{10,1... | collective-permute-start | bytes 1572872 | tf_op jit(solution)/shard_map/ppermute | solution.py:345
  61.9 17.4 %collective-permute-start.11 = (f32[16,64,128]{2,1,0:T(8,128)S(1)}, f32[16,64,128]{2,1,0:T(8,128)S(1)}, u32[]{:S(2)}, u32[]{:S(2)}) collective-permute-start(f32[16,64,128]{2,1,0:T(8,128)S(1)} %get-tuple-element.53), channel_id=1, source_target_pairs={{0,3},{1,0},{2,1},{3,2},{4,7},{5,4},{6,5},{7,6},{8,11},{9,8},{10,9... | collective-permute-start | bytes 1572872 | tf_op jit(solution)/shard_map/ppermute | solution.py:345
  65.2 17.8 %collective-permute-start.14 = (f32[16,64,128]{2,1,0:T(8,128)S(1)}, f32[16,64,128]{2,1,0:T(8,128)S(1)}, u32[]{:S(2)}, u32[]{:S(2)}) collective-permute-start(f32[16,64,128]{2,1,0:T(8,128)S(1)} %get-tuple-element.57), channel_id=1, source_target_pairs={{0,1},{1,2},{2,3},{3,0},{4,5},{5,6},{6,7},{7,4},{8,9},{9,10},{10,1... | collective-permute-start | bytes 1572872 | tf_op jit(solution)/shard_map/ppermute | solution.py:345
  68.2 22.1 %collective-permute-start.16 = (f32[16,64,128]{2,1,0:T(8,128)S(1)}, f32[16,64,128]{2,1,0:T(8,128)S(1)}, u32[]{:S(2)}, u32[]{:S(2)}) collective-permute-start(f32[16,64,128]{2,1,0:T(8,128)S(1)} %add.192), channel_id=1, source_target_pairs={{0,3},{1,0},{2,1},{3,2},{4,7},{5,4},{6,5},{7,6},{8,11},{9,8},{10,9... | collective-permute-start | bytes 1572872 | tf_op jit(solution)/shard_map/ppermute | solution.py:345
  72.0 21.7 %collective-permute-start.13 = (f32[16,64,128]{2,1,0:T(8,128)S(1)}, f32[16,64,128]{2,1,0:T(8,128)S(1)}, u32[]{:S(2)}, u32[]{:S(2)}) collective-permute-start(f32[16,64,128]{2,1,0:T(8,128)S(1)} %add.191), channel_id=1, source_target_pairs={{0,1},{1,2},{2,3},{3,0},{4,5},{5,6},{6,7},{7,4},{8,9},{9,10},{10,1... | collective-permute-start | bytes 1572872 | tf_op jit(solution)/shard_map/ppermute | solution.py:345
  93.8 14.9 %collective-permute-start.19 = (f32[16,64,128]{2,1,0:T(8,128)S(1)}, f32[16,64,128]{2,1,0:T(8,128)S(1)}, u32[]{:S(2)}, u32[]{:S(2)}) collective-permute-start(f32[16,64,128]{2,1,0:T(8,128)S(1)} %add_add_fusion.rest_1_), channel_id=1, source_target_pairs={{0,3},{1,0},{2,1},{3,2},{4,7},{5,4},{6,5},{7,6},{8,11},{9,8},{10,9... | collective-permute-start | bytes 1572872 | tf_op jit(solution)/shard_map/ppermute | solution.py:345
  94.3 16.1 %collective-permute-start.17 = (f32[16,64,128]{2,1,0:T(8,128)S(1)}, f32[16,64,128]{2,1,0:T(8,128)S(1)}, u32[]{:S(2)}, u32[]{:S(2)}) collective-permute-start(f32[16,64,128]{2,1,0:T(8,128)S(1)} %add_add_fusion.1.rest_0_), channel_id=1, source_target_pairs={{0,1},{1,2},{2,3},{3,0},{4,5},{5,6},{6,7},{7,4},{8,9},{9,10},{10,1... | collective-permute-start | bytes 1572872 | tf_op jit(solution)/shard_map/ppermute | solution.py:345
  96.1 25.6 %collective-permute-start.22 = (f32[16,64,128]{2,1,0:T(8,128)S(1)}, f32[16,64,128]{2,1,0:T(8,128)S(1)}, u32[]{:S(2)}, u32[]{:S(2)}) collective-permute-start(f32[16,64,128]{2,1,0:T(8,128)S(1)} %add_add_fusion.rest_1_), channel_id=1, source_target_pairs={{0,1},{1,2},{2,3},{3,0},{4,5},{5,6},{6,7},{7,4},{8,9},{9,10},{10,1... | collective-permute-start | bytes 1572872 | tf_op jit(solution)/shard_map/ppermute | solution.py:345
  96.2 25.5 %collective-permute-start.21 = (f32[16,64,128]{2,1,0:T(8,128)S(1)}, f32[16,64,128]{2,1,0:T(8,128)S(1)}, u32[]{:S(2)}, u32[]{:S(2)}) collective-permute-start(f32[16,64,128]{2,1,0:T(8,128)S(1)} %add_add_fusion.1.rest_0_), channel_id=1, source_target_pairs={{0,3},{1,0},{2,1},{3,2},{4,7},{5,4},{6,5},{7,6},{8,11},{9,8},{10,9... | collective-permute-start | bytes 1572872 | tf_op jit(solution)/shard_map/ppermute | solution.py:345
  108.7 20.9 %collective-permute-start.20 = (f32[16,64,128]{2,1,0:T(8,128)S(1)}, f32[16,64,128]{2,1,0:T(8,128)S(1)}, u32[]{:S(2)}, u32[]{:S(2)}) collective-permute-start(f32[16,64,128]{2,1,0:T(8,128)S(1)} %collective-permute-done.19.rest_0_), channel_id=1, source_target_pairs={{0,3},{1,0},{2,1},{3,2},{4,7},{5,4},{6,5},{7,6},{8,11},{9,8},{10,9... | collective-permute-start | bytes 1572872 | tf_op jit(solution)/shard_map/ppermute | solution.py:345
  110.4 21.0 %collective-permute-start.18 = (f32[16,64,128]{2,1,0:T(8,128)S(1)}, f32[16,64,128]{2,1,0:T(8,128)S(1)}, u32[]{:S(2)}, u32[]{:S(2)}) collective-permute-start(f32[16,64,128]{2,1,0:T(8,128)S(1)} %collective-permute-done.17.rest_1_), channel_id=1, source_target_pairs={{0,1},{1,2},{2,3},{3,0},{4,5},{5,6},{6,7},{7,4},{8,9},{9,10},{10,1... | collective-permute-start | bytes 1572872 | tf_op jit(solution)/shard_map/ppermute | solution.py:345
  136.7 10.3 %collective-permute-start.24 = (f32[4,72,128]{2,1,0:T(8,128)S(1)}, f32[4,72,128]{2,1,0:T(8,128)S(1)}, u32[]{:S(2)}, u32[]{:S(2)}) collective-permute-start(f32[4,72,128]{2,1,0:T(8,128)S(1)} %get-tuple-element.94), channel_id=1, source_target_pairs={{0,8},{4,12},{8,16},{12,20},{16,24},{20,28},{24,0},{28,4},{32,40},... | collective-permute-start | bytes 442376 | tf_op jit(solution)/shard_map/ppermute | solution.py:355
  136.8 10.2 %collective-permute-start.25 = (f32[4,72,128]{2,1,0:T(8,128)S(1)}, f32[4,72,128]{2,1,0:T(8,128)S(1)}, u32[]{:S(2)}, u32[]{:S(2)}) collective-permute-start(f32[4,72,128]{2,1,0:T(8,128)S(1)} %get-tuple-element.96), channel_id=1, source_target_pairs={{0,24},{4,28},{8,0},{12,4},{16,8},{20,12},{24,16},{28,20},{32,56},... | collective-permute-start | bytes 442376 | tf_op jit(solution)/shard_map/ppermute | solution.py:355
  172.8 14.9 %collective-permute-start.38 = (f32[16,64,128]{2,1,0:T(8,128)S(1)}, f32[16,64,128]{2,1,0:T(8,128)S(1)}, u32[]{:S(2)}, u32[]{:S(2)}) collective-permute-start(f32[16,64,128]{2,1,0:T(8,128)S(1)} %get-tuple-element.77), channel_id=1, source_target_pairs={{0,3},{1,0},{2,1},{3,2},{4,7},{5,4},{6,5},{7,6},{8,11},{9,8},{10,9... | collective-permute-start | bytes 1572872 | tf_op jit(solution)/shard_map/ppermute | solution.py:345
  172.9 16.1 %collective-permute-start.35 = (f32[16,64,128]{2,1,0:T(8,128)S(1)}, f32[16,64,128]{2,1,0:T(8,128)S(1)}, u32[]{:S(2)}, u32[]{:S(2)}) collective-permute-start(f32[16,64,128]{2,1,0:T(8,128)S(1)} %get-tuple-element.73), channel_id=1, source_target_pairs={{0,1},{1,2},{2,3},{3,0},{4,5},{5,6},{6,7},{7,4},{8,9},{9,10},{10,1... | collective-permute-start | bytes 1572872 | tf_op jit(solution)/shard_map/ppermute | solution.py:345
  180.9 18.0 %collective-permute-start.34 = (f32[16,64,128]{2,1,0:T(8,128)S(1)}, f32[16,64,128]{2,1,0:T(8,128)S(1)}, u32[]{:S(2)}, u32[]{:S(2)}) collective-permute-start(f32[16,64,128]{2,1,0:T(8,128)S(1)} %get-tuple-element.71), channel_id=1, source_target_pairs={{0,3},{1,0},{2,1},{3,2},{4,7},{5,4},{6,5},{7,6},{8,11},{9,8},{10,9... | collective-permute-start | bytes 1572872 | tf_op jit(solution)/shard_map/ppermute | solution.py:345
  182.3 17.9 %collective-permute-start.37 = (f32[16,64,128]{2,1,0:T(8,128)S(1)}, f32[16,64,128]{2,1,0:T(8,128)S(1)}, u32[]{:S(2)}, u32[]{:S(2)}) collective-permute-start(f32[16,64,128]{2,1,0:T(8,128)S(1)} %get-tuple-element.75), channel_id=1, source_target_pairs={{0,1},{1,2},{2,3},{3,0},{4,5},{5,6},{6,7},{7,4},{8,9},{9,10},{10,1... | collective-permute-start | bytes 1572872 | tf_op jit(solution)/shard_map/ppermute | solution.py:345
  187.8 21.1 %collective-permute-start.39 = (f32[16,64,128]{2,1,0:T(8,128)S(1)}, f32[16,64,128]{2,1,0:T(8,128)S(1)}, u32[]{:S(2)}, u32[]{:S(2)}) collective-permute-start(f32[16,64,128]{2,1,0:T(8,128)S(1)} %add.205), channel_id=1, source_target_pairs={{0,3},{1,0},{2,1},{3,2},{4,7},{5,4},{6,5},{7,6},{8,11},{9,8},{10,9... | collective-permute-start | bytes 1572872 | tf_op jit(solution)/shard_map/ppermute | solution.py:345
  189.1 21.1 %collective-permute-start.36 = (f32[16,64,128]{2,1,0:T(8,128)S(1)}, f32[16,64,128]{2,1,0:T(8,128)S(1)}, u32[]{:S(2)}, u32[]{:S(2)}) collective-permute-start(f32[16,64,128]{2,1,0:T(8,128)S(1)} %add.204), channel_id=1, source_target_pairs={{0,1},{1,2},{2,3},{3,0},{4,5},{5,6},{6,7},{7,4},{8,9},{9,10},{10,1... | collective-permute-start | bytes 1572872 | tf_op jit(solution)/shard_map/ppermute | solution.py:345
  210.9 26.6 %collective-permute-start.50 = (f32[32,64,128]{2,1,0:T(8,128)S(1)}, f32[32,64,128]{2,1,0:T(8,128)S(1)}, u32[]{:S(2)}, u32[]{:S(2)}) collective-permute-start(f32[32,64,128]{2,1,0:T(8,128)S(1)} %shard_map.93.own.refs_0_), channel_id=1, source_target_pairs={{0,1},{1,2},{2,3},{3,0},{4,5},{5,6},{6,7},{7,4},{8,9},{9,10},{10,1... | collective-permute-start | bytes 3145736 | tf_op jit(solution)/shard_map/ppermute | solution.py:345
  211.4 26.0 %collective-permute-start.51 = (f32[32,64,128]{2,1,0:T(8,128)S(1)}, f32[32,64,128]{2,1,0:T(8,128)S(1)}, u32[]{:S(2)}, u32[]{:S(2)}) collective-permute-start(f32[32,64,128]{2,1,0:T(8,128)S(1)} %shard_map.93.own.refs_0_), channel_id=1, source_target_pairs={{0,3},{1,0},{2,1},{3,2},{4,7},{5,4},{6,5},{7,6},{8,11},{9,8},{10,9... | collective-permute-start | bytes 3145736 | tf_op jit(solution)/shard_map/ppermute | solution.py:345
  237.5 12.6 %collective-permute-start.52 = (f32[16,64,128]{2,1,0:T(8,128)S(1)}, f32[16,64,128]{2,1,0:T(8,128)S(1)}, u32[]{:S(2)}, u32[]{:S(2)}) collective-permute-start(f32[16,64,128]{2,1,0:T(8,128)S(1)} %slice.121), channel_id=1, source_target_pairs={{0,1},{1,2},{2,3},{3,0},{4,5},{5,6},{6,7},{7,4},{8,9},{9,10},{10,1... | collective-permute-start | bytes 1572872 | tf_op jit(solution)/shard_map/ppermute | solution.py:345
  238.4 11.8 %collective-permute-start.53 = (f32[16,64,128]{2,1,0:T(8,128)S(1)}, f32[16,64,128]{2,1,0:T(8,128)S(1)}, u32[]{:S(2)}, u32[]{:S(2)}) collective-permute-start(f32[16,64,128]{2,1,0:T(8,128)S(1)} %slice.122), channel_id=1, source_target_pairs={{0,3},{1,0},{2,1},{3,2},{4,7},{5,4},{6,5},{7,6},{8,11},{9,8},{10,9... | collective-permute-start | bytes 1572872 | tf_op jit(solution)/shard_map/ppermute | solution.py:345
  (33 other events, 174.2 us)
where the time goes:
time: 254 us; the launch traced here: 252 us
  waiting for transfers between devices  120 us (47%)
  starting transfers between devices  69.3 us (27%)
  Pallas kernels  54.7 us (22%)
  local copies, waits for them, and re-layouts  4.27 us (2%)
  other arithmetic  3.61 us (1%)
    ppermute x25, waiting for transfers between devices, user_move(): return lax.ppermute(value, 'user', [(s, (s + by) % 4) for s in range(4)])  69.8 us
    ppermute x29, waiting for transfers between devices, item_move(): return lax.ppermute(value, 'item', pairs)  50.1 us
    ppermute x25, starting transfers between devices, user_move(): return lax.ppermute(value, 'user', [(s, (s + by) % 4) for s in range(4)])  34.9 us
    ppermute x29, starting transfers between devices, item_move(): return lax.ppermute(value, 'item', pairs)  34.3 us
    pallas_call x6, Pallas kernels, back_product(): pl.pallas_call(functools.partial(back_kernel, first, last, shift, sizes),...  17.1 us
    pallas_call x3, Pallas kernels, forth_product(): pl.pallas_call(functools.partial(forth_kernel, first, last, shift, len(pi...  10.8 us
    pallas_call x1, Pallas kernels, first_product(): pl.pallas_call(first_kernel, out_shape=(jax.ShapeDtypeStruct((UB, K, TB),...  8.89 us
    pallas_call x1, Pallas kernels, inverse_beside(): pl.pallas_call(inverse_beside_kernel, out_shape=jax.ShapeDtypeStruct((K,...  5.88 us
  transfers between devices with their start and end apart: 54, of which 41 were waited for; matrix products, arithmetic and copies ran while one was open for 1% of the time, Pallas kernels for 14%

commit v1 on v0

--- a/solution.py
+++ b/solution.py
@@ -66,15 +66,27 @@
     return core * 16 + x * 4 + y
 
 
-def first_kernel(upos, item, tiles, lengths, panel, users, stacked):
+def first_kernel(tiles, user_in, item_in, lengths_in, panel_in, users, stacked, where, user, item, lengths, panel, sems):
     step = pl.program_id(0)
+    spot = lax.axis_index("item")
 
     @pl.when(step == 0)
     def _():
+        pairs = (panel_in, panel), (lengths_in, lengths), (user_in, user), (item_in, item)
+        copies = [
+            pltpu.make_async_copy(source, target, sems.at[number])
+            for number, (source, target) in enumerate(pairs)
+        ]
+        for copy in copies:
+            copy.start()
         users[...] = jnp.zeros_like(users)
+        rows = lax.broadcasted_iota(jnp.int32, where.shape, 0)
+        where[...] = jnp.where(rows == 0, spot, lax.axis_index("user"))
+        for copy in copies:
+            copy.wait()
 
     columns = lax.broadcasted_iota(jnp.int32, (TB, TB), 1)
-    ends = lengths[...].T
+    ends = lengths[pl.ds(pl.multiple_of(step * GROUP, GROUP), GROUP)].T
     parts = []
     for t in range(GROUP):
         n = step * GROUP + t
@@ -82,34 +94,37 @@
         both = jnp.concatenate(split2(masked), axis=0)
         stacked[t] = both
         block = panel[:, pl.ds(pl.multiple_of(item[n] * TB, TB), TB)]
-        parts.append((upos[n], times_nt(block, both)))
-    for spot, value in parts:
-        users[spot] += value
-
-
-def first_product(upos, item, tiles, lengths, panel_t):
+        parts.append((place_of(user[n], spot), times_nt(block, both)))
+    for at, value in parts:
+        users[at] += value
+
+
+def first_product(user, item, tiles, lengths, panel_t):
     return pl.pallas_call(
         first_kernel,
         out_shape=(
             jax.ShapeDtypeStruct((UB, K, TB), F32),
-            pltpu.VMEM((NT, 2 * TB, TB), BF16),
+            jax.ShapeDtypeStruct((NT, 2 * TB, TB), BF16),
+            jax.ShapeDtypeStruct((8, 2 * TB), jnp.int32),
         ),
-        grid_spec=pltpu.PrefetchScalarGridSpec(
-            num_scalar_prefetch=2,
-            grid=(NT // GROUP,),
-            in_specs=[
-                pl.BlockSpec((GROUP, TB, TB), lambda s, *_: (s, 0, 0)),
-                pl.BlockSpec((GROUP, TB), lambda s, *_: (s, 0)),
-                pl.BlockSpec((K, IB * TB), lambda s, *_: (0, 0)),
-            ],
-            out_specs=[
-                pl.BlockSpec((UB, K, TB), lambda s, *_: (0, 0, 0)),
-                pl.BlockSpec((GROUP, 2 * TB, TB), lambda s, *_: (s, 0, 0)),
-            ],
-        ),
-        cost_estimate=cost(13.8),
+        grid=(NT // GROUP,),
+        in_specs=[pl.BlockSpec((GROUP, TB, TB), lambda s: (s, 0, 0))]
+        + [pl.BlockSpec(memory_space=pltpu.HBM)] * 4,
+        out_specs=[
+            pl.BlockSpec((UB, K, TB), lambda s: (0, 0, 0)),
+            pl.BlockSpec((GROUP, 2 * TB, TB), lambda s: (s, 0, 0)),
+            pl.BlockSpec((8, 2 * TB), lambda s: (0, 0)),
+        ],
+        scratch_shapes=[
+            pltpu.SMEM((NT,), jnp.int32),
+            pltpu.SMEM((NT,), jnp.int32),
+            pltpu.VMEM((NT, TB), jnp.int32),
+            pltpu.VMEM((K, IB * TB), F32),
+            pltpu.SemaphoreType.DMA((4,)),
+        ],
+        cost_estimate=cost(10.0),
         compiler_params=pltpu.CompilerParams(vmem_limit_bytes=28 * MIB),
-    )(upos, item, tiles, lengths, panel_t)
+    )(*(pltpu.with_memory_space_constraint(x, pltpu.HBM) for x in (tiles, user, item, lengths, panel_t)))
 
 
 def each_tile(first, last, lists, stacked, total, use):
@@ -425,17 +440,16 @@
     tiles = tiles.reshape(NT, TB, TB)
     user_block = tile_user.reshape(NT)
     item_block = tile_item.reshape(NT)
-    spot = lax.axis_index("item")
-    z = lax.axis_index("user")
-
+    part, stacked, where = first_product(
+        user_block, item_block, tiles, row_lengths.reshape(NT, TB), start_panel.T
+    )
+    upos = place_of(user_block, where[0, :NT])
+    ipos = item_places(item_block, where[1, :NT])
+    places = place_of(jnp.arange(UB, dtype=jnp.int32), where[0, :UB])
+    lists = tile_lists(upos, ipos, places)
     halves = (0, 0), (0, 1), (3, 0), (3, 1), (1, 0), (1, 1), (2, 0), (2, 1)
     quarters, odd = (jnp.array(column, jnp.int32) for column in zip(*halves))
-    base = ((z + quarters) % 4) * (QB * TB) + odd * (HB * TB)
-    upos, places = place_of(user_block, spot), place_of(jnp.arange(UB, dtype=jnp.int32), spot)
-    ipos = item_places(item_block, z)
-    upos, ipos, places, base = lax.optimization_barrier((upos, ipos, places, base))
-    part, stacked = first_product(upos, item_block, tiles, row_lengths.reshape(NT, TB), start_panel.T)
-    lists = tile_lists(upos, ipos, places)
+    base = ((where[1, :8] + quarters) % 4) * (QB * TB) + odd * (HB * TB)
     users = sum_over_item(part)
     terms = scatter(users, lists, stacked)
     own_a, own_b = (terms[0] + terms[1]) + terms[2], (terms[3] + terms[4]) + terms[5]

time: 254 us -> 249 us (0.980)
  local copies, waits for them, and re-layouts: 4.27 us -> 0.53 us
    unnamed x12 -> x14, local copies, waits for them, and re-layouts: 3.83 us -> 0.09 us
  transfers between devices with their start and end apart: 54 -> 54, of which waited for: 41 -> 42; matrix products, arithmetic and copies ran while one was open for 1% -> 1% of each run, Pallas kernels for 14% -> 13%
where the time goes in v1:
time: 249 us; the launch traced here: 247 us
  waiting for transfers between devices  119 us (48%)
  starting transfers between devices  69.6 us (28%)
  Pallas kernels  55.9 us (22%)
    ppermute x25, waiting for transfers between devices, user_move(): return lax.ppermute(value, 'user', [(s, (s + by) % 4) for s in range(4)])  70.5 us
    ppermute x29, waiting for transfers between devices, item_move(): return lax.ppermute(value, 'item', pairs)  48.7 us
    ppermute x25, starting transfers between devices, user_move(): return lax.ppermute(value, 'user', [(s, (s + by) % 4) for s in range(4)])  35 us
    ppermute x29, starting transfers between devices, item_move(): return lax.ppermute(value, 'item', pairs)  34.6 us
    pallas_call x6, Pallas kernels, back_product(): pl.pallas_call(functools.partial(back_kernel, first, last, shift, sizes),...  16.9 us
    pallas_call x1, Pallas kernels, first_product(): pl.pallas_call(first_kernel, out_shape=(jax.ShapeDtypeStruct((UB, K, TB),...  10.7 us
    pallas_call x3, Pallas kernels, forth_product(): pl.pallas_call(functools.partial(forth_kernel, first, last, shift, len(pi...  10.2 us
    pallas_call x1, Pallas kernels, inverse_beside(): pl.pallas_call(inverse_beside_kernel, out_shape=jax.ShapeDtypeStruct((K,...  5.88 us
  transfers between devices with their start and end apart: 54, of which 42 were waited for; matrix products, arithmetic and copies ran while one was open for 1% of the time, Pallas kernels for 13%

profile of v1, /device:TPU:0, one launch (start us, length us, event | category | flops | bytes accessed | tf_op | source)
XLA Modules:
  0.0 247.5 jit_solution(2719634845511896826)
XLA Ops:
  0.0 10.7 %shard_map.82 = (f32[32,64,128]{2,1,0:T(8,128)S(1)}, bf16[192,256,128]{2,1,0:T(8,128)(2,1)S(1)}, s32[8,256]{1,0:T(8,128)S(1)}) custom-call(f32[192,128,128]{2,1,0:T(8,128)} %bitcast.81, s32[192]{0:T(256)} %bitcast.87, s32[192]{0:T(256)} %bitcast.84, s32[192,128]{1,0:T(8,128)} %bitcast.83, f32[64,16384]{1,0:T(8,128)} %bitcast.82), custom_call_target="tpu_custom_call" | custom-call | bytes 35000000 | tf_op jit(solution)/shard_map/pallas_call | solution.py:103
  23.6 3.3 %collective-permute-start.4 = (f32[4,64,128]{2,1,0:T(8,128)S(1)}, f32[4,64,128]{2,1,0:T(8,128)S(1)}, u32[]{:S(2)}, u32[]{:S(2)}) collective-permute-start(f32[4,64,128]{2,1,0:T(8,128)S(1)} %fusion.4), channel_id=1, source_target_pairs={{0,64},{4,68},{8,72},{12,76},{16,80},{20,84},{24,88},{28,92},{32,9... | collective-permute-start | bytes 393224 | tf_op jit(solution)/shard_map/ppermute | solution.py:370
  48.5 3.3 %collective-permute-start.15 = (f32[16,64,128]{2,1,0:T(8,128)S(1)}, f32[16,64,128]{2,1,0:T(8,128)S(1)}, u32[]{:S(2)}, u32[]{:S(2)}) collective-permute-start(f32[16,64,128]{2,1,0:T(8,128)S(1)} %get-tuple-element.53), channel_id=1, source_target_pairs={{0,3},{1,0},{2,1},{3,2},{4,7},{5,4},{6,5},{7,6},{8,11},{9,8},{10,9... | collective-permute-start | bytes 1572872 | tf_op jit(solution)/shard_map/ppermute | solution.py:360
  51.8 3.5 %shard_map.83 = (f32[16,64,128]{2,1,0:T(8,128)S(1)}, f32[16,64,128]{2,1,0:T(8,128)S(1)}, f32[16,64,128]{2,1,0:T(8,128)S(1)}, f32[16,64,128]{2,1,0:T(8,128)S(1)}) custom-call(s32[640]{0:T(1024)S(1)} %pad_add_fusion.lists, f32[32,64,128]{2,1,0:T(8,128)S(1)} %constant_dynamic-update-slice_fusion.users, bf16[192,256,128]{2,1,0:T(8,128)(2,1)S(1)} %get-tuple-element.44.stacked), custom_call_target="tpu_custom_call" | custom-call | bytes 17710000 | tf_op jit(solution)/shard_map/pallas_call | solution.py:163
  57.4 3.7 %collective-permute-start.11 = (f32[16,64,128]{2,1,0:T(8,128)S(1)}, f32[16,64,128]{2,1,0:T(8,128)S(1)}, u32[]{:S(2)}, u32[]{:S(2)}) collective-permute-start(f32[16,64,128]{2,1,0:T(8,128)S(1)} %get-tuple-element.47), channel_id=1, source_target_pairs={{0,3},{1,0},{2,1},{3,2},{4,7},{5,4},{6,5},{7,6},{8,11},{9,8},{10,9... | collective-permute-start | bytes 1572872 | tf_op jit(solution)/shard_map/ppermute | solution.py:360
  64.2 3.8 %collective-permute-start.16 = (f32[16,64,128]{2,1,0:T(8,128)S(1)}, f32[16,64,128]{2,1,0:T(8,128)S(1)}, u32[]{:S(2)}, u32[]{:S(2)}) collective-permute-start(f32[16,64,128]{2,1,0:T(8,128)S(1)} %add.267), channel_id=1, source_target_pairs={{0,3},{1,0},{2,1},{3,2},{4,7},{5,4},{6,5},{7,6},{8,11},{9,8},{10,9... | collective-permute-start | bytes 1572872 | tf_op jit(solution)/shard_map/ppermute | solution.py:360
  68.1 7.3 %collective-permute-done.11 = f32[16,64,128]{2,1,0:T(8,128)S(1)} collective-permute-done((f32[16,64,128]{2,1,0:T(8,128)S(1)}, f32[16,64,128]{2,1,0:T(8,128)S(1)}, u32[]{:S(2)}, u32[]{:S(2)}) %collective-permute-start.11) | collective-permute-done | bytes 524320 | tf_op jit(solution)/shard_map/ppermute | solution.py:360
  75.3 3.7 %collective-permute-done.14 = f32[16,64,128]{2,1,0:T(8,128)S(1)} collective-permute-done((f32[16,64,128]{2,1,0:T(8,128)S(1)}, f32[16,64,128]{2,1,0:T(8,128)S(1)}, u32[]{:S(2)}, u32[]{:S(2)}) %collective-permute-start.14) | collective-permute-done | bytes 524320 | tf_op jit(solution)/shard_map/ppermute | solution.py:360
  79.1 6.7 %collective-permute-done.16 = f32[16,64,128]{2,1,0:T(8,128)S(1)} collective-permute-done((f32[16,64,128]{2,1,0:T(8,128)S(1)}, f32[16,64,128]{2,1,0:T(8,128)S(1)}, u32[]{:S(2)}, u32[]{:S(2)}) %collective-permute-start.16) | collective-permute-done | bytes 524320 | tf_op jit(solution)/shard_map/ppermute | solution.py:360
  85.8 3.4 %collective-permute-done.13 = f32[16,64,128]{2,1,0:T(8,128)S(1)} collective-permute-done((f32[16,64,128]{2,1,0:T(8,128)S(1)}, f32[16,64,128]{2,1,0:T(8,128)S(1)}, u32[]{:S(2)}, u32[]{:S(2)}) %collective-permute-start.13) | collective-permute-done | bytes 524320 | tf_op jit(solution)/shard_map/ppermute | solution.py:360
  94.8 9.4 %collective-permute-done.19.rest_0_ = f32[16,64,128]{2,1,0:T(8,128)S(1)} collective-permute-done((f32[16,64,128]{2,1,0:T(8,128)S(1)}, f32[16,64,128]{2,1,0:T(8,128)S(1)}, u32[]{:S(2)}, u32[]{:S(2)}) %collective-permute-start.19) | collective-permute-done | bytes 524320 | tf_op jit(solution)/shard_map/ppermute | solution.py:360
  109.1 8.0 %collective-permute-done.22.rest_3_ = f32[16,64,128]{2,1,0:T(8,128)S(1)} collective-permute-done((f32[16,64,128]{2,1,0:T(8,128)S(1)}, f32[16,64,128]{2,1,0:T(8,128)S(1)}, u32[]{:S(2)}, u32[]{:S(2)}) %collective-permute-start.22) | collective-permute-done | bytes 524320 | tf_op jit(solution)/shard_map/ppermute | solution.py:360
  117.1 4.0 %shard_map.87 = (f32[32,64,128]{2,1,0:T(8,128)S(1)}, f32[64,64]{1,0:T(8,128)S(1)}) custom-call(s32[640]{0:T(1024)S(1)} %pad_add_fusion.lists, bf16[192,256,128]{2,1,0:T(8,128)(2,1)S(1)} %get-tuple-element.44.stacked, f32[16,64,128]{2,1,0:T(8,128)S(1)} %collective-permute-done.19.rest_0_, f32[16,64,128]{2,1,0:T(8,128)S(1)} %collective-permute-done.17.rest_1_, ...), custom_call_target="tpu_custom_call" | custom-call | bytes 21700000 | tf_op jit(solution)/shard_map/pallas_call | solution.py:217
  121.1 3.5 %collective-permute-done.20.rest_1_ = f32[16,64,128]{2,1,0:T(8,128)S(1)} collective-permute-done((f32[16,64,128]{2,1,0:T(8,128)S(1)}, f32[16,64,128]{2,1,0:T(8,128)S(1)}, u32[]{:S(2)}, u32[]{:S(2)}) %collective-permute-start.20) | collective-permute-done | bytes 524320 | tf_op jit(solution)/shard_map/ppermute | solution.py:360
  126.3 3.5 %shard_map.88 = f32[32,72,128]{2,1,0:T(8,128)S(1)} custom-call(s32[640]{0:T(1024)S(1)} %pad_add_fusion.lists, bf16[192,256,128]{2,1,0:T(8,128)(2,1)S(1)} %get-tuple-element.44.stacked, f32[16,64,128]{2,1,0:T(8,128)S(1)} %collective-permute-done.18.rest_0_, f32[16,64,128]{2,1,0:T(8,128)S(1)} %collective-permute-done.20.rest_1_, ...), custom_call_target="tpu_custom_call" | custom-call | bytes 16099999 | tf_op jit(solution)/shard_map/pallas_call | solution.py:217
  135.7 6.8 %collective-permute-done.24 = f32[4,72,128]{2,1,0:T(8,128)S(1)} collective-permute-done((f32[4,72,128]{2,1,0:T(8,128)S(1)}, f32[4,72,128]{2,1,0:T(8,128)S(1)}, u32[]{:S(2)}, u32[]{:S(2)}) %collective-permute-start.24) | collective-permute-done | bytes 147488 | tf_op jit(solution)/shard_map/ppermute | solution.py:370
  146.6 3.3 %collective-permute-done.28 = f32[4,72,128]{2,1,0:T(8,128)S(1)} collective-permute-done((f32[4,72,128]{2,1,0:T(8,128)S(1)}, f32[4,72,128]{2,1,0:T(8,128)S(1)}, u32[]{:S(2)}, u32[]{:S(2)}) %collective-permute-start.28) | collective-permute-done | bytes 147488 | tf_op jit(solution)/shard_map/ppermute | solution.py:370
  156.6 4.1 %collective-permute-done.30 = f32[4,72,128]{2,1,0:T(8,128)S(1)} collective-permute-done((f32[4,72,128]{2,1,0:T(8,128)S(1)}, f32[4,72,128]{2,1,0:T(8,128)S(1)}, u32[]{:S(2)}, u32[]{:S(2)}) %collective-permute-start.30) | collective-permute-done | bytes 147488 | tf_op jit(solution)/shard_map/ppermute | solution.py:370
  171.3 3.5 %shard_map.90 = (f32[16,64,128]{2,1,0:T(8,128)S(1)}, f32[16,64,128]{2,1,0:T(8,128)S(1)}, f32[16,64,128]{2,1,0:T(8,128)S(1)}, f32[16,64,128]{2,1,0:T(8,128)S(1)}) custom-call(s32[640]{0:T(1024)S(1)} %pad_add_fusion.lists, f32[32,72,128]{2,1,0:T(8,128)S(1)} %constant_dynamic-update-slice_fusion.5.users, bf16[192,256,128]{2,1,0:T(8,128)(2,1)S(1)} %get-tuple-element.44.stacked), custom_call_target="tpu_custom_call" | custom-call | bytes 17710000 | tf_op jit(solution)/shard_map/pallas_call | solution.py:163
  178.9 5.2 %collective-permute-done.38 = f32[16,64,128]{2,1,0:T(8,128)S(1)} collective-permute-done((f32[16,64,128]{2,1,0:T(8,128)S(1)}, f32[16,64,128]{2,1,0:T(8,128)S(1)}, u32[]{:S(2)}, u32[]{:S(2)}) %collective-permute-start.38) | collective-permute-done | bytes 524320 | tf_op jit(solution)/shard_map/ppermute | solution.py:360
  186.7 5.9 %shard_map.89.inverse = f32[64,64]{1,0:T(8,128)S(1)} custom-call(s32[640]{0:T(1024)S(1)} %pad_add_fusion.lists, f32[32,72,128]{2,1,0:T(8,128)S(1)} %constant_dynamic-update-slice_fusion.5.users), custom_call_target="tpu_custom_call" | custom-call | bytes 24150000 | tf_op jit(solution)/shard_map/pallas_call | solution.py:280
  196.7 8.2 %collective-permute-done.39.refs_5_ = f32[16,64,128]{2,1,0:T(8,128)S(1)} collective-permute-done((f32[16,64,128]{2,1,0:T(8,128)S(1)}, f32[16,64,128]{2,1,0:T(8,128)S(1)}, u32[]{:S(2)}, u32[]{:S(2)}) %collective-permute-start.39) | collective-permute-done | bytes 524320 | tf_op jit(solution)/shard_map/ppermute | solution.py:360
  236.5 5.3 %shard_map.95.inverse = f32[64,64]{1,0:T(8,128)S(1)} custom-call(f32[64,64]{1,0:T(8,128)S(1)} %add_add_fusion.2.gram), custom_call_target="tpu_custom_call" | custom-call | bytes 23450000 | tf_op jit(solution)/shard_map/pallas_call | solution.py:263
  241.8 3.3 %shard_map.96.refs_2_ = f32[64,16384]{1,0:T(8,128)} custom-call(s32[6]{0:T(128)S(1)} %bitcast.80, f32[64,64]{1,0:T(8,128)S(1)} %shard_map.95.inverse, f32[32,64,128]{2,1,0:T(8,128)S(1)} %shard_map.93.own.refs_0_, f32[32,64,128]{2,1,0:T(8,128)S(1)} %collective-permute-done.50.refs_1_, f32[32,64,128]{2,1,0:T(8,128)S(1)} %collective-permute-done.51.refs_2_), custom_call_target="tpu_custom_call" | custom-call | bytes 14000000 | tf_op jit(solution)/shard_map/pallas_call | solution.py:344
  (160 shorter events, 123.4 us)
Async XLA Ops:
  48.5 15.6 %collective-permute-start.15 = (f32[16,64,128]{2,1,0:T(8,128)S(1)}, f32[16,64,128]{2,1,0:T(8,128)S(1)}, u32[]{:S(2)}, u32[]{:S(2)}) collective-permute-start(f32[16,64,128]{2,1,0:T(8,128)S(1)} %get-tuple-element.53), channel_id=1, source_target_pairs={{0,3},{1,0},{2,1},{3,2},{4,7},{5,4},{6,5},{7,6},{8,11},{9,8},{10,9... | collective-permute-start | bytes 1572872 | tf_op jit(solution)/shard_map/ppermute | solution.py:360
  51.8 16.1 %collective-permute-start.12 = (f32[16,64,128]{2,1,0:T(8,128)S(1)}, f32[16,64,128]{2,1,0:T(8,128)S(1)}, u32[]{:S(2)}, u32[]{:S(2)}) collective-permute-start(f32[16,64,128]{2,1,0:T(8,128)S(1)} %get-tuple-element.49), channel_id=1, source_target_pairs={{0,1},{1,2},{2,3},{3,0},{4,5},{5,6},{6,7},{7,4},{8,9},{9,10},{10,1... | collective-permute-start | bytes 1572872 | tf_op jit(solution)/shard_map/ppermute | solution.py:360
  57.4 18.0 %collective-permute-start.11 = (f32[16,64,128]{2,1,0:T(8,128)S(1)}, f32[16,64,128]{2,1,0:T(8,128)S(1)}, u32[]{:S(2)}, u32[]{:S(2)}) collective-permute-start(f32[16,64,128]{2,1,0:T(8,128)S(1)} %get-tuple-element.47), channel_id=1, source_target_pairs={{0,3},{1,0},{2,1},{3,2},{4,7},{5,4},{6,5},{7,6},{8,11},{9,8},{10,9... | collective-permute-start | bytes 1572872 | tf_op jit(solution)/shard_map/ppermute | solution.py:360
  61.1 17.9 %collective-permute-start.14 = (f32[16,64,128]{2,1,0:T(8,128)S(1)}, f32[16,64,128]{2,1,0:T(8,128)S(1)}, u32[]{:S(2)}, u32[]{:S(2)}) collective-permute-start(f32[16,64,128]{2,1,0:T(8,128)S(1)} %get-tuple-element.51), channel_id=1, source_target_pairs={{0,1},{1,2},{2,3},{3,0},{4,5},{5,6},{6,7},{7,4},{8,9},{9,10},{10,1... | collective-permute-start | bytes 1572872 | tf_op jit(solution)/shard_map/ppermute | solution.py:360
  64.2 21.6 %collective-permute-start.16 = (f32[16,64,128]{2,1,0:T(8,128)S(1)}, f32[16,64,128]{2,1,0:T(8,128)S(1)}, u32[]{:S(2)}, u32[]{:S(2)}) collective-permute-start(f32[16,64,128]{2,1,0:T(8,128)S(1)} %add.267), channel_id=1, source_target_pairs={{0,3},{1,0},{2,1},{3,2},{4,7},{5,4},{6,5},{7,6},{8,11},{9,8},{10,9... | collective-permute-start | bytes 1572872 | tf_op jit(solution)/shard_map/ppermute | solution.py:360
  68.0 21.2 %collective-permute-start.13 = (f32[16,64,128]{2,1,0:T(8,128)S(1)}, f32[16,64,128]{2,1,0:T(8,128)S(1)}, u32[]{:S(2)}, u32[]{:S(2)}) collective-permute-start(f32[16,64,128]{2,1,0:T(8,128)S(1)} %add.266), channel_id=1, source_target_pairs={{0,1},{1,2},{2,3},{3,0},{4,5},{5,6},{6,7},{7,4},{8,9},{9,10},{10,1... | collective-permute-start | bytes 1572872 | tf_op jit(solution)/shard_map/ppermute | solution.py:360
  89.3 14.9 %collective-permute-start.19 = (f32[16,64,128]{2,1,0:T(8,128)S(1)}, f32[16,64,128]{2,1,0:T(8,128)S(1)}, u32[]{:S(2)}, u32[]{:S(2)}) collective-permute-start(f32[16,64,128]{2,1,0:T(8,128)S(1)} %add_add_fusion.rest_1_), channel_id=1, source_target_pairs={{0,3},{1,0},{2,1},{3,2},{4,7},{5,4},{6,5},{7,6},{8,11},{9,8},{10,9... | collective-permute-start | bytes 1572872 | tf_op jit(solution)/shard_map/ppermute | solution.py:360
  89.7 16.1 %collective-permute-start.17 = (f32[16,64,128]{2,1,0:T(8,128)S(1)}, f32[16,64,128]{2,1,0:T(8,128)S(1)}, u32[]{:S(2)}, u32[]{:S(2)}) collective-permute-start(f32[16,64,128]{2,1,0:T(8,128)S(1)} %add_add_fusion.1.rest_0_), channel_id=1, source_target_pairs={{0,1},{1,2},{2,3},{3,0},{4,5},{5,6},{6,7},{7,4},{8,9},{9,10},{10,1... | collective-permute-start | bytes 1572872 | tf_op jit(solution)/shard_map/ppermute | solution.py:360
  91.5 25.6 %collective-permute-start.22 = (f32[16,64,128]{2,1,0:T(8,128)S(1)}, f32[16,64,128]{2,1,0:T(8,128)S(1)}, u32[]{:S(2)}, u32[]{:S(2)}) collective-permute-start(f32[16,64,128]{2,1,0:T(8,128)S(1)} %add_add_fusion.rest_1_), channel_id=1, source_target_pairs={{0,1},{1,2},{2,3},{3,0},{4,5},{5,6},{6,7},{7,4},{8,9},{9,10},{10,1... | collective-permute-start | bytes 1572872 | tf_op jit(solution)/shard_map/ppermute | solution.py:360
  91.6 25.5 %collective-permute-start.21 = (f32[16,64,128]{2,1,0:T(8,128)S(1)}, f32[16,64,128]{2,1,0:T(8,128)S(1)}, u32[]{:S(2)}, u32[]{:S(2)}) collective-permute-start(f32[16,64,128]{2,1,0:T(8,128)S(1)} %add_add_fusion.1.rest_0_), channel_id=1, source_target_pairs={{0,3},{1,0},{2,1},{3,2},{4,7},{5,4},{6,5},{7,6},{8,11},{9,8},{10,9... | collective-permute-start | bytes 1572872 | tf_op jit(solution)/shard_map/ppermute | solution.py:360
  104.2 20.4 %collective-permute-start.20 = (f32[16,64,128]{2,1,0:T(8,128)S(1)}, f32[16,64,128]{2,1,0:T(8,128)S(1)}, u32[]{:S(2)}, u32[]{:S(2)}) collective-permute-start(f32[16,64,128]{2,1,0:T(8,128)S(1)} %collective-permute-done.19.rest_0_), channel_id=1, source_target_pairs={{0,3},{1,0},{2,1},{3,2},{4,7},{5,4},{6,5},{7,6},{8,11},{9,8},{10,9... | collective-permute-start | bytes 1572872 | tf_op jit(solution)/shard_map/ppermute | solution.py:360
  105.9 20.5 %collective-permute-start.18 = (f32[16,64,128]{2,1,0:T(8,128)S(1)}, f32[16,64,128]{2,1,0:T(8,128)S(1)}, u32[]{:S(2)}, u32[]{:S(2)}) collective-permute-start(f32[16,64,128]{2,1,0:T(8,128)S(1)} %collective-permute-done.17.rest_1_), channel_id=1, source_target_pairs={{0,1},{1,2},{2,3},{3,0},{4,5},{5,6},{6,7},{7,4},{8,9},{9,10},{10,1... | collective-permute-start | bytes 1572872 | tf_op jit(solution)/shard_map/ppermute | solution.py:360
  132.1 10.3 %collective-permute-start.24 = (f32[4,72,128]{2,1,0:T(8,128)S(1)}, f32[4,72,128]{2,1,0:T(8,128)S(1)}, u32[]{:S(2)}, u32[]{:S(2)}) collective-permute-start(f32[4,72,128]{2,1,0:T(8,128)S(1)} %get-tuple-element.90), channel_id=1, source_target_pairs={{0,8},{4,12},{8,16},{12,20},{16,24},{20,28},{24,0},{28,4},{32,40},... | collective-permute-start | bytes 442376 | tf_op jit(solution)/shard_map/ppermute | solution.py:370
  132.2 10.2 %collective-permute-start.25 = (f32[4,72,128]{2,1,0:T(8,128)S(1)}, f32[4,72,128]{2,1,0:T(8,128)S(1)}, u32[]{:S(2)}, u32[]{:S(2)}) collective-permute-start(f32[4,72,128]{2,1,0:T(8,128)S(1)} %get-tuple-element.92), channel_id=1, source_target_pairs={{0,24},{4,28},{8,0},{12,4},{16,8},{20,12},{24,16},{28,20},{32,56},... | collective-permute-start | bytes 442376 | tf_op jit(solution)/shard_map/ppermute | solution.py:370
  169.2 14.9 %collective-permute-start.38 = (f32[16,64,128]{2,1,0:T(8,128)S(1)}, f32[16,64,128]{2,1,0:T(8,128)S(1)}, u32[]{:S(2)}, u32[]{:S(2)}) collective-permute-start(f32[16,64,128]{2,1,0:T(8,128)S(1)} %get-tuple-element.71), channel_id=1, source_target_pairs={{0,3},{1,0},{2,1},{3,2},{4,7},{5,4},{6,5},{7,6},{8,11},{9,8},{10,9... | collective-permute-start | bytes 1572872 | tf_op jit(solution)/shard_map/ppermute | solution.py:360
  169.3 16.2 %collective-permute-start.35 = (f32[16,64,128]{2,1,0:T(8,128)S(1)}, f32[16,64,128]{2,1,0:T(8,128)S(1)}, u32[]{:S(2)}, u32[]{:S(2)}) collective-permute-start(f32[16,64,128]{2,1,0:T(8,128)S(1)} %get-tuple-element.67), channel_id=1, source_target_pairs={{0,1},{1,2},{2,3},{3,0},{4,5},{5,6},{6,7},{7,4},{8,9},{9,10},{10,1... | collective-permute-start | bytes 1572872 | tf_op jit(solution)/shard_map/ppermute | solution.py:360
  176.9 18.5 %collective-permute-start.34 = (f32[16,64,128]{2,1,0:T(8,128)S(1)}, f32[16,64,128]{2,1,0:T(8,128)S(1)}, u32[]{:S(2)}, u32[]{:S(2)}) collective-permute-start(f32[16,64,128]{2,1,0:T(8,128)S(1)} %get-tuple-element.65), channel_id=1, source_target_pairs={{0,3},{1,0},{2,1},{3,2},{4,7},{5,4},{6,5},{7,6},{8,11},{9,8},{10,9... | collective-permute-start | bytes 1572872 | tf_op jit(solution)/shard_map/ppermute | solution.py:360
  178.7 18.0 %collective-permute-start.37 = (f32[16,64,128]{2,1,0:T(8,128)S(1)}, f32[16,64,128]{2,1,0:T(8,128)S(1)}, u32[]{:S(2)}, u32[]{:S(2)}) collective-permute-start(f32[16,64,128]{2,1,0:T(8,128)S(1)} %get-tuple-element.69), channel_id=1, source_target_pairs={{0,1},{1,2},{2,3},{3,0},{4,5},{5,6},{6,7},{7,4},{8,9},{9,10},{10,1... | collective-permute-start | bytes 1572872 | tf_op jit(solution)/shard_map/ppermute | solution.py:360
  184.2 20.6 %collective-permute-start.39 = (f32[16,64,128]{2,1,0:T(8,128)S(1)}, f32[16,64,128]{2,1,0:T(8,128)S(1)}, u32[]{:S(2)}, u32[]{:S(2)}) collective-permute-start(f32[16,64,128]{2,1,0:T(8,128)S(1)} %add.280), channel_id=1, source_target_pairs={{0,3},{1,0},{2,1},{3,2},{4,7},{5,4},{6,5},{7,6},{8,11},{9,8},{10,9... | collective-permute-start | bytes 1572872 | tf_op jit(solution)/shard_map/ppermute | solution.py:360
  185.6 20.5 %collective-permute-start.36 = (f32[16,64,128]{2,1,0:T(8,128)S(1)}, f32[16,64,128]{2,1,0:T(8,128)S(1)}, u32[]{:S(2)}, u32[]{:S(2)}) collective-permute-start(f32[16,64,128]{2,1,0:T(8,128)S(1)} %add.279), channel_id=1, source_target_pairs={{0,1},{1,2},{2,3},{3,0},{4,5},{5,6},{6,7},{7,4},{8,9},{9,10},{10,1... | collective-permute-start | bytes 1572872 | tf_op jit(solution)/shard_map/ppermute | solution.py:360
  206.9 26.1 %collective-permute-start.50 = (f32[32,64,128]{2,1,0:T(8,128)S(1)}, f32[32,64,128]{2,1,0:T(8,128)S(1)}, u32[]{:S(2)}, u32[]{:S(2)}) collective-permute-start(f32[32,64,128]{2,1,0:T(8,128)S(1)} %shard_map.93.own.refs_0_), channel_id=1, source_target_pairs={{0,1},{1,2},{2,3},{3,0},{4,5},{5,6},{6,7},{7,4},{8,9},{9,10},{10,1... | collective-permute-start | bytes 3145736 | tf_op jit(solution)/shard_map/ppermute | solution.py:360
  207.4 25.6 %collective-permute-start.51 = (f32[32,64,128]{2,1,0:T(8,128)S(1)}, f32[32,64,128]{2,1,0:T(8,128)S(1)}, u32[]{:S(2)}, u32[]{:S(2)}) collective-permute-start(f32[32,64,128]{2,1,0:T(8,128)S(1)} %shard_map.93.own.refs_0_), channel_id=1, source_target_pairs={{0,3},{1,0},{2,1},{3,2},{4,7},{5,4},{6,5},{7,6},{8,11},{9,8},{10,9... | collective-permute-start | bytes 3145736 | tf_op jit(solution)/shard_map/ppermute | solution.py:360
  233.0 12.2 %collective-permute-start.52 = (f32[16,64,128]{2,1,0:T(8,128)S(1)}, f32[16,64,128]{2,1,0:T(8,128)S(1)}, u32[]{:S(2)}, u32[]{:S(2)}) collective-permute-start(f32[16,64,128]{2,1,0:T(8,128)S(1)} %slice.137), channel_id=1, source_target_pairs={{0,1},{1,2},{2,3},{3,0},{4,5},{5,6},{6,7},{7,4},{8,9},{9,10},{10,1... | collective-permute-start | bytes 1572872 | tf_op jit(solution)/shard_map/ppermute | solution.py:360
  233.7 11.5 %collective-permute-start.53 = (f32[16,64,128]{2,1,0:T(8,128)S(1)}, f32[16,64,128]{2,1,0:T(8,128)S(1)}, u32[]{:S(2)}, u32[]{:S(2)}) collective-permute-start(f32[16,64,128]{2,1,0:T(8,128)S(1)} %slice.138), channel_id=1, source_target_pairs={{0,3},{1,0},{2,1},{3,2},{4,7},{5,4},{6,5},{7,6},{8,11},{9,8},{10,9... | collective-permute-start | bytes 1572872 | tf_op jit(solution)/shard_map/ppermute | solution.py:360
  (34 other events, 232.8 us)
